TPU v7x, 32 devices: a whole 2x2x4 slice. The times are simulated.
32 devices in a mesh: samp: 8 (over z, y), var: 4 (over x, core).
Axes of the slice: x: 2, y: 2, z: 4, core: 2. Of those that a mesh axis runs over, the one named last changes fastest.
Arguments:
- genotypes: int32 [2048, 4096], P('samp', 'var'), may hold values from -1 to 2, as said below
- ancestry: float32 [16, 2048], P(None, 'samp'), may hold values from 0.05 to 4, as said below
- frequency: float32 [16, 4096], P(None, 'var'), may hold values from 0.05 to 0.95
Outputs:
- new_ancestry: float32 [16, 2048], P(None, 'samp')
- new_frequency: float32 [16, 4096], P(None, 'var')
Inputs may be any that keep to these rules, and one draw needn't show every extreme that they name: `genotypes`: A dosage of 0, 1 or 2 alternate alleles, or -1 for a missing genotype. `ancestry`: positive weights.
All inputs are finite; a program needn't handle non-finite values.
Results may differ from a plain program's by a relative error of at most 0.0003.
Values sent between devices are 32-bit elements; how exact they have to be, the bound alone decides.
A program may use at most 64 MiB of HBM per device.

v0:
```python
import jax
import jax.numpy as jnp
from jax import lax
from jax.sharding import PartitionSpec as P

ITERS = 4
HIGH = lax.Precision.HIGHEST


def contract(left, right, left_dim, right_dim):
    return lax.dot_general(
        left,
        right,
        (((left_dim,), (right_dim,)), ((), ())),
        precision=HIGH,
        preferred_element_type=jnp.float32,
    )


def shards(genotypes, ancestry, frequency):
    present = (genotypes >= 0).astype(jnp.float32)
    dosage = jnp.maximum(genotypes, 0).astype(jnp.float32)
    weight_ref = present * dosage
    weight_alt = present * (2.0 - dosage)
    fraction = ancestry / jnp.sum(ancestry, axis=0, keepdims=True)
    for sweep in range(ITERS):
        expected = contract(fraction, frequency, 0, 0)
        ratio_ref = weight_ref / expected
        ratio_alt = weight_alt / (1.0 - expected)
        partial_value = contract(frequency, ratio_ref, 1, 1) + contract(
            1.0 - frequency, ratio_alt, 1, 1
        )
        total = lax.psum(partial_value, "var")
        weighted = fraction * total
        fraction = weighted / jnp.sum(weighted, axis=0, keepdims=True)
        expected = contract(fraction, frequency, 0, 0)
        ratio_ref = weight_ref / expected
        ratio_alt = weight_alt / (1.0 - expected)
        term_ref = contract(fraction, ratio_ref, 1, 0)
        term_alt = contract(fraction, ratio_alt, 1, 0)
        sum_ref, sum_alt = lax.psum((term_ref, term_alt), "samp")
        upper = frequency * sum_ref
        lower = (1.0 - frequency) * sum_alt
        frequency = upper / (upper + lower)
    return (fraction, frequency)


def solution(mesh):
    return jax.shard_map(
        shards,
        mesh=mesh,
        in_specs=(P("samp", "var"), P(None, "samp"), P(None, "var")),
        out_specs=(P(None, "samp"), P(None, "var")),
        check_vma=False,
    )
```

profile of v0, /device:TPU:0, one launch (start us, length us, event | category | flops | bytes accessed | tf_op | source)
XLA Modules:
  0.0 370.3 jit_solution(9430064719370559565)
XLA Ops:
  7.2 0.0 copy-start.1
  7.2 0.0 copy-start.3
  7.2 0.0 all-reduce.15.cloned.1.call-start
  7.2 0.8 reduce_sum.45
  8.0 0.0 copy-done.1
  8.1 0.0 copy-start
  8.1 1.9 fusion.36
  10.0 0.0 copy-done.3
  10.0 0.0 copy-done
  10.0 1.1 convolution_bitcast_fusion
  11.1 1.1 convolution_add_fusion.3
  12.2 12.7 %psum.84 = f32[16,256]{1,0:T(8,128)S(1)} all-reduce(f32[16,256]{1,0:T(8,128)S(1)} %convolution_add_fusion.3), channel_id=1, replica_groups=mesh['samp'=8,'var'=4] {'var'}, use_global_device_ids=true, to_apply=%region_1.0 | all-reduce | flops 4096 | bytes 32768 | tf_op jit(solution)/shard_map/psum | solution.py:33
  24.9 1.0 fusion.52
  25.9 1.5 fusion.15
  27.5 1.5 fusion.12
  28.9 0.0 all-reduce.15.cloned.1.call-update
  29.0 0.0 all-reduce.13.cloned.1.call-start
  29.0 70.3 %all-reduce.15.cloned.1.call-done = (f32[16,1024]{1,0:T(8,128)}, f32[16,1024]{1,0:T(8,128)}) async-done(((f32[16,1024]{1,0:T(8,128)}, f32[16,1024]{1,0:T(8,128)}), (f32[16,1024]{1,0:T(8,128)}, f32[16,1024]{1,0:T(8,128)})) %all-reduce.15.cloned.1.call-update) | async-done | bytes 131088 | tf_op jit(solution)/shard_map/psum | solution.py:41
  99.3 0.9 add_divide_fusion.3
  100.2 1.0 fusion.53
  101.3 1.0 fusion.10
  102.3 1.1 convolution_add_fusion.2
  103.4 10.1 %psum.87 = f32[16,256]{1,0:T(8,128)S(1)} all-reduce(f32[16,256]{1,0:T(8,128)S(1)} %convolution_add_fusion.2), channel_id=1, replica_groups=mesh['samp'=8,'var'=4] {'var'}, use_global_device_ids=true, to_apply=%region_5.0 | all-reduce | flops 4096 | bytes 32768 | tf_op jit(solution)/shard_map/psum | solution.py:33
  113.5 1.0 fusion.48
  114.5 1.5 fusion.16
  116.1 1.5 fusion.8
  117.5 0.0 all-reduce.13.cloned.1.call-update
  117.6 0.2 all-reduce.11.cloned.1.call-start
  117.8 69.2 %all-reduce.13.cloned.1.call-done = (f32[16,1024]{1,0:T(8,128)}, f32[16,1024]{1,0:T(8,128)}) async-done(((f32[16,1024]{1,0:T(8,128)}, f32[16,1024]{1,0:T(8,128)}), (f32[16,1024]{1,0:T(8,128)}, f32[16,1024]{1,0:T(8,128)})) %all-reduce.13.cloned.1.call-update) | async-done | bytes 131088 | tf_op jit(solution)/shard_map/psum | solution.py:41
  187.0 0.9 add_divide_fusion.2
  187.8 1.0 fusion.47
  188.9 1.0 fusion.6
  189.9 1.1 convolution_add_fusion.1
  191.0 10.1 %psum.90 = f32[16,256]{1,0:T(8,128)S(1)} all-reduce(f32[16,256]{1,0:T(8,128)S(1)} %convolution_add_fusion.1), channel_id=1, replica_groups=mesh['samp'=8,'var'=4] {'var'}, use_global_device_ids=true, to_apply=%region_9.0 | all-reduce | flops 4096 | bytes 32768 | tf_op jit(solution)/shard_map/psum | solution.py:33
  201.1 1.0 fusion.54
  202.2 1.5 fusion.17
  203.7 1.5 fusion.4
  205.2 0.0 all-reduce.11.cloned.1.call-update
  205.2 0.0 all-reduce.9.cloned.1.call-start
  205.2 69.4 %all-reduce.11.cloned.1.call-done = (f32[16,1024]{1,0:T(8,128)}, f32[16,1024]{1,0:T(8,128)}) async-done(((f32[16,1024]{1,0:T(8,128)}, f32[16,1024]{1,0:T(8,128)}), (f32[16,1024]{1,0:T(8,128)}, f32[16,1024]{1,0:T(8,128)})) %all-reduce.11.cloned.1.call-update) | async-done | bytes 131088 | tf_op jit(solution)/shard_map/psum | solution.py:41
  274.6 0.9 add_divide_fusion.1
  275.5 1.0 fusion.55
  276.5 1.0 fusion.2
  277.6 1.1 convolution_add_fusion
  278.6 10.1 %psum.93 = f32[16,256]{1,0:T(8,128)S(1)} all-reduce(f32[16,256]{1,0:T(8,128)S(1)} %convolution_add_fusion), channel_id=1, replica_groups=mesh['samp'=8,'var'=4] {'var'}, use_global_device_ids=true, to_apply=%region_13.0 | all-reduce | flops 4096 | bytes 32768 | tf_op jit(solution)/shard_map/psum | solution.py:33
  288.8 0.0 copy-start.2
  288.8 1.0 fusion.56
  289.8 1.5 fusion.18
  291.4 0.0 copy-done.2
  291.4 1.5 fusion
  292.8 0.0 all-reduce.9.cloned.1.call-update
  292.9 69.4 %all-reduce.9.cloned.1.call-done = (f32[16,1024]{1,0:T(8,128)}, f32[16,1024]{1,0:T(8,128)}) async-done(((f32[16,1024]{1,0:T(8,128)}, f32[16,1024]{1,0:T(8,128)}), (f32[16,1024]{1,0:T(8,128)}, f32[16,1024]{1,0:T(8,128)})) %all-reduce.9.cloned.1.call-update) | async-done | bytes 131088 | tf_op jit(solution)/shard_map/psum | solution.py:41
  362.2 1.5 add_divide_fusion
  (7 shorter events, 0.1 us)
Async XLA Ops:
  7.2 0.9 copy-start.1
  7.2 2.8 copy-start.3
  7.2 92.1 %all-reduce.15.cloned.1.call-start = ((), (), s32[]{:S(2)}) async-start(), calls=%async_computation.3 | async-start | bytes 262144 | tf_op jit(solution)/shard_map/psum | solution.py:41
  8.1 2.0 copy-start
  29.0 158.0 %all-reduce.13.cloned.1.call-start = ((), (), s32[]{:S(2)}) async-start(), calls=%async_computation.2 | async-start | bytes 262144 | tf_op jit(solution)/shard_map/psum | solution.py:41
  117.6 157.1 %all-reduce.11.cloned.1.call-start = ((), (), s32[]{:S(2)}) async-start(), calls=%async_computation.1 | async-start | bytes 262144 | tf_op jit(solution)/shard_map/psum | solution.py:41
  205.2 157.1 %all-reduce.9.cloned.1.call-start = ((), (), s32[]{:S(2)}) async-start(), calls=%async_computation | async-start | bytes 262144 | tf_op jit(solution)/shard_map/psum | solution.py:41
  288.8 2.6 copy-start.2
Sparse Core Ops, SparseCore 0:
  29.1 70.2 all-reduce.14
  117.7 69.2 all-reduce.12
  205.3 69.2 all-reduce.10
  293.0 69.2 all-reduce.8
where the time goes:
time: 371 us; the launch traced here: 370 us
  waiting for transfers between devices  278 us (75%)
  blocking collectives  43 us (12%)
  matrix products  29.6 us (8%)
  between operations  13.9 us (4%)
  other arithmetic  5.13 us (1%)
    psum x4, waiting for transfers between devices, shards(): sum_ref, sum_alt = lax.psum((term_ref, term_alt), 'samp')  278 us
    psum x4, blocking collectives, shards(): total = lax.psum(partial_value, 'var')  43 us
    dot_general x24, matrix products, contract(): lax.dot_general(left, right, (((left_dim,), (right_dim,)), ((), ())), pre...  29.6 us
  transfers between devices with their start and end apart: 4, of which 4 were waited for; matrix products, arithmetic and copies ran while one was open for 0% of the time, Pallas kernels for 0%

commit v1 on v0

--- a/solution.py
+++ b/solution.py
@@ -30,7 +30,9 @@
         partial_value = contract(frequency, ratio_ref, 1, 1) + contract(
             1.0 - frequency, ratio_alt, 1, 1
         )
-        total = lax.psum(partial_value, "var")
+        total = partial_value
+        for hop in (1, 2):
+            total = total + lax.ppermute(total, "var", [(dev, dev ^ hop) for dev in range(4)])
         weighted = fraction * total
         fraction = weighted / jnp.sum(weighted, axis=0, keepdims=True)
         expected = contract(fraction, frequency, 0, 0)

time: 371 us -> 350 us (0.943)
  blocking collectives: 43 us -> 0 us
  waiting for transfers between devices: 278 us -> 292 us
  starting transfers between devices: 0.34 us -> 8.25 us
    psum x4 -> x0, blocking collectives: 43 us -> none  [shards(): total = lax.psum(partial_value, 'var')]
    ppermute x0 -> x8, waiting for transfers between devices: none -> 12.9 us  [shards(): lax.ppermute(total, 'var', [(dev, dev ^ hop) for dev in range(4)])]
    ppermute x0 -> x8, starting transfers between devices: none -> 7.9 us  [shards(): lax.ppermute(total, 'var', [(dev, dev ^ hop) for dev in range(4)])]
  transfers between devices with their start and end apart: 4 -> 12, of which waited for: 4 -> 12; matrix products, arithmetic and copies ran while one was open for 0% -> 0% of each run, Pallas kernels for 0% -> 0%
where the time goes in v1:
time: 350 us; the launch traced here: 349 us
  waiting for transfers between devices  292 us (83%)
  matrix products  29.6 us (8%)
  between operations  13.9 us (4%)
  starting transfers between devices  8.25 us (2%)
  other arithmetic  5.15 us (1%)
    psum x4, waiting for transfers between devices, shards(): sum_ref, sum_alt = lax.psum((term_ref, term_alt), 'samp')  279 us
    dot_general x24, matrix products, contract(): lax.dot_general(left, right, (((left_dim,), (right_dim,)), ((), ())), pre...  29.6 us
    ppermute x8, waiting for transfers between devices, shards(): lax.ppermute(total, 'var', [(dev, dev ^ hop) for dev in range(4)])  12.9 us
    ppermute x8, starting transfers between devices, shards(): lax.ppermute(total, 'var', [(dev, dev ^ hop) for dev in range(4)])  7.9 us
  transfers between devices with their start and end apart: 12, of which 12 were waited for; matrix products, arithmetic and copies ran while one was open for 0% of the time, Pallas kernels for 0%

profile of v1, /device:TPU:0, one launch (start us, length us, event | category | flops | bytes accessed | tf_op | source)
XLA Modules:
  0.0 349.2 jit_solution(90104206432959598)
XLA Ops:
  7.2 0.0 copy-start.1
  7.2 0.0 copy-start.3
  7.2 0.0 all-reduce.15.cloned.1.call-start
  7.2 0.8 reduce_sum.45
  8.0 0.0 copy-done.1
  8.1 0.0 copy-start
  8.1 1.9 fusion.35
  10.0 0.0 copy-done.3
  10.0 0.0 copy-done
  10.0 1.1 convolution_bitcast_fusion
  11.1 1.1 convolution_add_fusion.3
  12.2 0.5 collective-permute-start
  12.7 0.8 collective-permute-done
  13.6 2.8 collective-permute-start.1
  16.4 1.7 collective-permute-done.1
  18.1 1.0 fusion.48
  19.2 1.5 fusion.15
  20.7 1.5 fusion.12
  22.2 0.0 all-reduce.15.cloned.1.call-update
  22.2 0.0 all-reduce.13.cloned.1.call-start
  22.2 71.8 %all-reduce.15.cloned.1.call-done = (f32[16,1024]{1,0:T(8,128)}, f32[16,1024]{1,0:T(8,128)}) async-done(((f32[16,1024]{1,0:T(8,128)}, f32[16,1024]{1,0:T(8,128)}), (f32[16,1024]{1,0:T(8,128)}, f32[16,1024]{1,0:T(8,128)})) %all-reduce.15.cloned.1.call-update) | async-done | bytes 131088 | tf_op jit(solution)/shard_map/psum | solution.py:43
  94.0 0.9 add_divide_fusion.3
  94.9 1.0 fusion.47
  95.9 1.0 fusion.10
  96.9 1.1 convolution_add_fusion.2
  98.0 0.1 collective-permute-start.2
  98.1 1.2 collective-permute-done.2
  99.3 1.5 collective-permute-start.3
  100.7 2.3 collective-permute-done.3
  103.1 1.0 fusion.50
  104.1 1.5 fusion.16
  105.6 1.5 fusion.8
  107.1 0.0 all-reduce.13.cloned.1.call-update
  107.1 0.2 all-reduce.11.cloned.1.call-start
  107.3 69.1 %all-reduce.13.cloned.1.call-done = (f32[16,1024]{1,0:T(8,128)}, f32[16,1024]{1,0:T(8,128)}) async-done(((f32[16,1024]{1,0:T(8,128)}, f32[16,1024]{1,0:T(8,128)}), (f32[16,1024]{1,0:T(8,128)}, f32[16,1024]{1,0:T(8,128)})) %all-reduce.13.cloned.1.call-update) | async-done | bytes 131088 | tf_op jit(solution)/shard_map/psum | solution.py:43
  176.4 0.9 add_divide_fusion.2
  177.3 1.0 fusion.51
  178.3 1.0 fusion.6
  179.3 1.1 convolution_add_fusion.1
  180.4 0.1 collective-permute-start.4
  180.5 1.2 collective-permute-done.4
  181.7 1.5 collective-permute-start.5
  183.1 2.3 collective-permute-done.5
  185.5 1.0 fusion.52
  186.5 1.5 fusion.17
  188.0 1.5 fusion.4
  189.5 0.0 all-reduce.11.cloned.1.call-update
  189.5 0.0 all-reduce.9.cloned.1.call-start
  189.5 69.2 %all-reduce.11.cloned.1.call-done = (f32[16,1024]{1,0:T(8,128)}, f32[16,1024]{1,0:T(8,128)}) async-done(((f32[16,1024]{1,0:T(8,128)}, f32[16,1024]{1,0:T(8,128)}), (f32[16,1024]{1,0:T(8,128)}, f32[16,1024]{1,0:T(8,128)})) %all-reduce.11.cloned.1.call-update) | async-done | bytes 131088 | tf_op jit(solution)/shard_map/psum | solution.py:43
  258.8 0.9 add_divide_fusion.1
  259.7 1.0 fusion.53
  260.7 1.0 fusion.2
  261.7 1.1 convolution_add_fusion
  262.8 0.1 collective-permute-start.6
  262.9 1.2 collective-permute-done.6
  264.1 1.5 collective-permute-start.7
  265.5 2.3 collective-permute-done.7
  267.8 0.0 copy-start.2
  267.8 1.0 fusion.54
  268.9 1.5 fusion.18
  270.4 1.5 fusion
  271.9 0.0 all-reduce.9.cloned.1.call-update
  271.9 69.3 %all-reduce.9.cloned.1.call-done = (f32[16,1024]{1,0:T(8,128)}, f32[16,1024]{1,0:T(8,128)}) async-done(((f32[16,1024]{1,0:T(8,128)}, f32[16,1024]{1,0:T(8,128)}), (f32[16,1024]{1,0:T(8,128)}, f32[16,1024]{1,0:T(8,128)})) %all-reduce.9.cloned.1.call-update) | async-done | bytes 131088 | tf_op jit(solution)/shard_map/psum | solution.py:43
  341.2 1.5 add_divide_fusion
  (12 shorter events, 0.1 us)
Async XLA Ops:
  7.2 0.9 copy-start.1
  7.2 2.8 copy-start.3
  7.2 86.8 %all-reduce.15.cloned.1.call-start = ((), (), s32[]{:S(2)}) async-start(), calls=%async_computation.3 | async-start | bytes 262144 | tf_op jit(solution)/shard_map/psum | solution.py:43
  8.1 2.0 copy-start
  12.2 1.3 collective-permute-start
  13.6 4.5 %collective-permute-start.1 = (f32[16,256]{1,0:T(8,128)S(1)}, f32[16,256]{1,0:T(8,128)S(1)}, u32[]{:S(2)}, u32[]{:S(2)}) collective-permute-start(f32[16,256]{1,0:T(8,128)S(1)} %add.65), channel_id=1, source_target_pairs={{0,2},{1,3},{2,0},{3,1},{4,6},{5,7},{6,4},{7,5},{8,10},{9,11},{10,... | collective-permute-start | bytes 49160 | tf_op jit(solution)/shard_map/ppermute | solution.py:35
  22.2 154.2 %all-reduce.13.cloned.1.call-start = ((), (), s32[]{:S(2)}) async-start(), calls=%async_computation.2 | async-start | bytes 262144 | tf_op jit(solution)/shard_map/psum | solution.py:43
  98.0 1.2 collective-permute-start.2
  99.3 3.7 %collective-permute-start.3 = (f32[16,256]{1,0:T(8,128)S(1)}, f32[16,256]{1,0:T(8,128)S(1)}, u32[]{:S(2)}, u32[]{:S(2)}) collective-permute-start(f32[16,256]{1,0:T(8,128)S(1)} %add.69), channel_id=1, source_target_pairs={{0,2},{1,3},{2,0},{3,1},{4,6},{5,7},{6,4},{7,5},{8,10},{9,11},{10,... | collective-permute-start | bytes 49160 | tf_op jit(solution)/shard_map/ppermute | solution.py:35
  107.1 151.7 %all-reduce.11.cloned.1.call-start = ((), (), s32[]{:S(2)}) async-start(), calls=%async_computation.1 | async-start | bytes 262144 | tf_op jit(solution)/shard_map/psum | solution.py:43
  180.4 1.2 collective-permute-start.4
  181.7 3.7 %collective-permute-start.5 = (f32[16,256]{1,0:T(8,128)S(1)}, f32[16,256]{1,0:T(8,128)S(1)}, u32[]{:S(2)}, u32[]{:S(2)}) collective-permute-start(f32[16,256]{1,0:T(8,128)S(1)} %add.73), channel_id=1, source_target_pairs={{0,2},{1,3},{2,0},{3,1},{4,6},{5,7},{6,4},{7,5},{8,10},{9,11},{10,... | collective-permute-start | bytes 49160 | tf_op jit(solution)/shard_map/ppermute | solution.py:35
  189.5 151.7 %all-reduce.9.cloned.1.call-start = ((), (), s32[]{:S(2)}) async-start(), calls=%async_computation | async-start | bytes 262144 | tf_op jit(solution)/shard_map/psum | solution.py:43
  262.8 1.2 collective-permute-start.6
  264.1 3.7 %collective-permute-start.7 = (f32[16,256]{1,0:T(8,128)S(1)}, f32[16,256]{1,0:T(8,128)S(1)}, u32[]{:S(2)}, u32[]{:S(2)}) collective-permute-start(f32[16,256]{1,0:T(8,128)S(1)} %add.77), channel_id=1, source_target_pairs={{0,2},{1,3},{2,0},{3,1},{4,6},{5,7},{6,4},{7,5},{8,10},{9,11},{10,... | collective-permute-start | bytes 49160 | tf_op jit(solution)/shard_map/ppermute | solution.py:35
  267.8 2.6 copy-start.2
Sparse Core Ops, SparseCore 0:
  22.3 71.6 all-reduce.14
  107.2 69.1 all-reduce.12
  189.6 69.1 all-reduce.10
  272.0 69.1 all-reduce.8
